TPU v7x, 256 devices: a whole 4x4x8 slice. The times are simulated.
256 devices in a mesh: rows: 16 (over z_lo, x, core), rep: 16 (over y, z_hi).
Axes of the slice: x: 4, y: 4, z: 8 (z_hi: 4, z_lo: 2; z = z_hi * 2 + z_lo), core: 2. Of those that a mesh axis runs over, the one named last changes fastest.
Arguments:
- node_features: bfloat16 [32768, 256], P(('rows', 'rep')), may hold values from -6 to 6
- adjacency: bfloat16 [256, 64, 128, 128], P('rows', 'rep'), may hold values from -0.078125 to 0.078125
- column_ids: int32 [256, 64], P('rows', 'rep'), may hold values from 0 to 15
- block_counts: int32 [256, 16], P('rows', 'rep'), may hold values from 1 to 4, 40 in all within a row
- weight_first: bfloat16 [256, 512], replicated, may hold values from -0.375 to 0.375
- weight_second: bfloat16 [512, 256], replicated, may hold values from -0.25 to 0.25
- cotangent: bfloat16 [32768, 256], P(('rows', 'rep')), may hold values from -6 to 6
Outputs:
- embedding: bfloat16 [32768, 256], P(('rows', 'rep'))
- grad_first: float32 [256, 512], replicated
- grad_second: float32 [512, 256], replicated
Inputs may be any that keep to these rules, and one draw needn't show every extreme that they name: `block_counts`: each row block has 40 live slots over its 16 groups; some group of some row block has all 4 live.
All inputs are finite; a program needn't handle non-finite values.
Results may differ from a plain program's by a relative error of at most 0.024.
Values may be sent and summed in bfloat16 or wider, within the bound.
A program may use at most 64 MiB of HBM per device.

v0:
```python
import math
import jax
import jax.numpy as jnp
from jax import lax
from jax.sharding import PartitionSpec as P

BS = 128


def slot_weights(adjacency, block_counts, slot):
    weights = adjacency[:, slot]
    live_rows = slot < block_counts[:, 0]
    return jnp.where(live_rows[:, None, None], weights, jnp.zeros_like(weights))


def aggregate(node_field, adjacency, column_ids, block_counts):
    feature_width = node_field.shape[1]
    gathered = lax.all_gather(node_field, "rows", axis=0, tiled=True)
    blocks_in = gathered.reshape(-1, BS, feature_width)
    row_blocks = column_ids.shape[0]
    partial_sum = jnp.zeros((row_blocks, BS, feature_width), jnp.float32)
    for slot in range(column_ids.shape[1]):
        weights = slot_weights(adjacency, block_counts, slot)
        picked = blocks_in[column_ids[:, slot]]
        partial_sum = partial_sum + jnp.einsum(
            "rij,rjf->rif", weights, picked, preferred_element_type=jnp.float32
        )
    return lax.psum_scatter(
        partial_sum.reshape(row_blocks * BS, feature_width).astype(jnp.bfloat16),
        "rep",
        scatter_dimension=0,
        tiled=True,
    ).astype(jnp.float32)


def transpose_aggregate(cotangent, adjacency, column_ids, block_counts):
    feature_width = cotangent.shape[1]
    row_blocks = column_ids.shape[0]
    gathered = lax.all_gather(cotangent, "rep", axis=0, tiled=True).reshape(
        row_blocks, BS, feature_width
    )
    col_blocks = lax.axis_size("rows") * (cotangent.shape[0] // BS)
    summed = jnp.zeros((col_blocks, BS, feature_width), jnp.float32)
    for slot in range(column_ids.shape[1]):
        weights = slot_weights(adjacency, block_counts, slot)
        terms = jnp.einsum("rij,rif->rjf", weights, gathered, preferred_element_type=jnp.float32)
        summed = summed.at[column_ids[:, slot]].add(terms)
    return lax.psum_scatter(
        summed.reshape(col_blocks * BS, feature_width).astype(jnp.bfloat16),
        "rows",
        scatter_dimension=0,
        tiled=True,
    ).astype(jnp.float32)


def shards(
    node_features, adjacency, column_ids, block_counts, weight_first, weight_second, cotangent
):
    contract = (((0,), (0,)), ((), ()))
    mixed_input = aggregate(node_features, adjacency, column_ids, block_counts).astype(jnp.bfloat16)
    pre_first = jnp.dot(mixed_input, weight_first, preferred_element_type=jnp.float32)
    hidden = jax.nn.silu(pre_first).astype(jnp.bfloat16)
    second_in = jnp.dot(hidden, weight_second, preferred_element_type=jnp.float32).astype(
        jnp.bfloat16
    )
    embedding = aggregate(second_in, adjacency, column_ids, block_counts).astype(jnp.bfloat16)
    upstream = transpose_aggregate(cotangent, adjacency, column_ids, block_counts).astype(
        jnp.bfloat16
    )
    node_total = node_features.shape[0] * lax.axis_size("rows") * lax.axis_size("rep")
    scale_factor = 1.0 / math.sqrt(node_total)
    local_second = lax.dot_general(hidden, upstream, contract, preferred_element_type=jnp.float32)
    back_hidden = lax.dot_general(
        upstream, weight_second, (((1,), (1,)), ((), ())), preferred_element_type=jnp.float32
    )
    sigmoid_gate = jax.nn.sigmoid(pre_first)
    back_pre = (back_hidden * sigmoid_gate * (1.0 + pre_first * (1.0 - sigmoid_gate))).astype(
        jnp.bfloat16
    )
    local_first = lax.dot_general(
        mixed_input, back_pre, contract, preferred_element_type=jnp.float32
    )
    grad_first, grad_second = lax.psum((local_first, local_second), ("rows", "rep"))
    return (embedding, grad_first * scale_factor, grad_second * scale_factor)


def solution(mesh):
    in_specs = (
        P(("rows", "rep"), None),
        P("rows", "rep", None, None),
        P("rows", "rep"),
        P("rows", "rep"),
        P(),
        P(),
        P(("rows", "rep"), None),
    )
    out_specs = (P(("rows", "rep"), None), P(), P())
    return jax.shard_map(shards, mesh=mesh, in_specs=in_specs, out_specs=out_specs, check_vma=False)
```

profile of v0, /device:TPU:2, one launch (start us, length us, event | category | flops | bytes accessed | tf_op | source)
XLA Modules:
  0.0 649.3 jit_solution(16340234801673374021)
XLA Ops:
  7.2 0.7 all-gather.4.cloned.1.call-update
  8.0 0.7 all-gather.8.cloned.1.call-update
  8.7 0.8 fusion.10
  9.6 0.7 compare_bitcast_fusion
  10.2 37.3 %all-gather.4.cloned.1.call-done = bf16[2048,256]{1,0:T(8,128)(2,1)} async-done(((bf16[128,256]{1,0:T(8,128)(2,1)}), bf16[2048,256]{1,0:T(8,128)(2,1)}) %all-gather.4.cloned.1.call-update) | async-done | bytes 1048592 | tf_op jit(solution)/shard_map/all_gather | solution.py:18
  47.6 2.9 gather_fusion.2
  50.5 1.6 gather_fusion
  52.1 1.6 gather_fusion.1
  53.7 1.6 gather_fusion.3
  55.3 1.8 fusion.21
  57.1 0.5 fusion.18
  57.6 0.7 copy-done.9
  58.3 0.5 fusion.15
  58.8 0.1 copy-done.6
  58.9 1.6 add_convert_fusion.1
  60.5 0.0 reduce-scatter.8.cloned.1.call-start
  60.6 43.4 %all-gather.8.cloned.1.call-done = bf16[2048,256]{1,0:T(8,128)(2,1)} async-done(((bf16[128,256]{1,0:T(8,128)(2,1)}), bf16[2048,256]{1,0:T(8,128)(2,1)}) %all-gather.8.cloned.1.call-update) | async-done | bytes 1048592 | tf_op jit(solution)/shard_map/all_gather | solution.py:39
  104.0 3.3 fusion.16
  107.3 0.2 broadcast_in_dim.78
  107.5 3.5 scatter_fusion
  111.1 3.1 fusion.13
  114.2 3.5 scatter_fusion.1
  117.7 3.1 fusion.19
  120.8 3.5 scatter_fusion.2
  124.4 3.1 fusion.22
  127.5 3.5 scatter_fusion.3
  131.0 1.1 convert_element_type.39
  132.2 0.0 all-gather.6.cloned.1.call-start
  132.2 58.8 %reduce-scatter.4.cloned.1.call-done = bf16[128,256]{1,0:T(8,128)(2,1)} async-done(((bf16[2048,256]{1,0:T(8,128)(2,1)}), bf16[128,256]{1,0:T(8,128)(2,1)}) %reduce-scatter.4.cloned.1.call-update) | async-done | bytes 65552 | tf_op jit(solution)/shard_map/reduce_scatter | solution.py:28
  191.1 1.1 fusion.23
  192.2 0.8 convolution_convert_fusion
  193.0 0.0 all-reduce.3.cloned.1.call-start
  193.1 58.3 %reduce-scatter.8.cloned.1.call-done = bf16[128,256]{1,0:T(8,128)(2,1)} async-done(((bf16[2048,256]{1,0:T(8,128)(2,1)}), bf16[128,256]{1,0:T(8,128)(2,1)}) %reduce-scatter.8.cloned.1.call-update) | async-done | bytes 65552 | tf_op jit(solution)/shard_map/reduce_scatter | solution.py:48
  251.4 1.9 fusion.12
  253.3 2.1 fusion.2
  255.5 34.7 %all-gather.6.cloned.1.call-done = bf16[2048,256]{1,0:T(8,128)(2,1)} async-done(((bf16[128,256]{1,0:T(8,128)(2,1)}), bf16[2048,256]{1,0:T(8,128)(2,1)}) %all-gather.6.cloned.1.call-update) | async-done | bytes 1048592 | tf_op jit(solution)/shard_map/all_gather | solution.py:18
  290.2 2.9 gather_fusion.6
  293.1 1.6 gather_fusion.4
  294.7 1.6 gather_fusion.5
  296.3 3.1 fusion.20
  299.4 1.8 fusion.17
  301.3 1.8 fusion.14
  303.1 1.7 gather_fusion.7
  304.8 4.8 add_convert_fusion
  309.5 243.3 %all-reduce.3.cloned.1.call-done = (f32[256,512]{1,0:T(8,128)}, f32[512,256]{1,0:T(8,128)}) async-done(((f32[256,512]{1,0:T(8,128)}, f32[512,256]{1,0:T(8,128)}), (f32[256,512]{1,0:T(8,128)}, f32[512,256]{1,0:T(8,128)})) %all-reduce.3.cloned.1.call-update) | async-done | bytes 1048592 | tf_op jit(solution)/shard_map/psum | solution.py:83
  552.9 1.9 broadcast_multiply_fusion.1
  554.7 1.9 broadcast_multiply_fusion
  556.6 85.8 %reduce-scatter.6.cloned.1.call-done = bf16[128,256]{1,0:T(8,128)(2,1)} async-done(((bf16[2048,256]{1,0:T(8,128)(2,1)}), bf16[128,256]{1,0:T(8,128)(2,1)}) %reduce-scatter.6.cloned.1.call-update) | async-done | bytes 65552 | tf_op jit(solution)/shard_map/reduce_scatter | solution.py:28
  (35 shorter events, 0.3 us)
Async XLA Ops:
  7.2 185.0 %copy-start = (bf16[512,256]{1,0:T(8,128)(2,1)S(1)}, bf16[512,256]{1,0:T(8,128)(2,1)}, u32[]{:S(2)}) copy-start(bf16[512,256]{1,0:T(8,128)(2,1)} %param.12) | copy-start | bytes 786436
  7.2 40.4 %all-gather.4.cloned.1.call-start = ((), (), s32[]{:S(2)}) async-start(), calls=%async_computation.3 | async-start | bytes 1114112 | tf_op jit(solution)/shard_map/all_gather | solution.py:18
  7.9 96.1 %all-gather.8.cloned.1.call-start = ((), (), s32[]{:S(2)}) async-start(), calls=%async_computation.7 | async-start | bytes 1114112 | tf_op jit(solution)/shard_map/all_gather | solution.py:39
  8.7 182.4 %reduce-scatter.4.cloned.1.call-start = ((), (), s32[]{:S(2)}) async-start(), calls=%async_computation.4 | async-start | bytes 1114112 | tf_op jit(solution)/shard_map/reduce_scatter | solution.py:28
  47.6 2.9 copy-start.4
  52.1 3.2 copy-start.1
  55.3 1.8 copy-start.8
  57.1 1.2 copy-start.9
  57.6 1.3 copy-start.6
  60.5 190.9 %reduce-scatter.8.cloned.1.call-start = ((), (), s32[]{:S(2)}) async-start(), calls=%async_computation.8 | async-start | bytes 1114112 | tf_op jit(solution)/shard_map/reduce_scatter | solution.py:48
  107.5 3.5 copy-start.5
  131.0 60.1 %copy-start.11 = (bf16[256,512]{1,0:T(8,128)(2,1)S(1)}, bf16[256,512]{1,0:T(8,128)(2,1)}, u32[]{:S(2)}) copy-start(bf16[256,512]{1,0:T(8,128)(2,1)} %param.11) | copy-start | bytes 786436
  132.2 158.0 %all-gather.6.cloned.1.call-start = ((), (), s32[]{:S(2)}) async-start(), calls=%async_computation.5 | async-start | bytes 1114112 | tf_op jit(solution)/shard_map/all_gather | solution.py:18
  191.1 62.3 %copy-start.12 = (bf16[128,256]{1,0:T(8,128)(2,1)S(1)}, bf16[128,256]{1,0:T(8,128)(2,1)}, u32[]{:S(2)}) copy-start(bf16[128,256]{1,0:T(8,128)(2,1)} %reduce-scatter.4.cloned.1.call-done) | copy-start | bytes 196612
  193.0 359.8 %all-reduce.3.cloned.1.call-start = ((), (), s32[]{:S(2)}) async-start(), calls=%async_computation.9 | async-start | bytes 2097152 | tf_op jit(solution)/shard_map/psum | solution.py:83
  255.4 387.0 %reduce-scatter.6.cloned.1.call-start = ((), (), s32[]{:S(2)}) async-start(), calls=%async_computation.6 | async-start | bytes 1114112 | tf_op jit(solution)/shard_map/reduce_scatter | solution.py:28
  290.2 2.9 copy-start.3
  293.1 3.2 copy-start.2
  296.3 3.1 copy-start.10
  299.4 1.8 copy-start.7
Sparse Core Ops, SparseCore 0:
  9.9 37.6 all-gather.3
  50.0 53.9 all-gather.7
  107.5 83.4 reduce-scatter.3
  193.6 57.7 reduce-scatter.7
  253.7 36.4 all-gather.5
  296.2 256.5 all-reduce.2
  557.3 85.0 reduce-scatter.5
where the time goes:
time: 650 us; the launch traced here: 649 us
  waiting for transfers between devices  563 us (87%)
  matrix products  34.5 us (5%)
  other arithmetic  20.4 us (3%)
  local copies, waits for them, and re-layouts  16.5 us (3%)
  between operations  14.3 us (2%)
    psum x1, waiting for transfers between devices, shards(): lax.psum((local_first, local_second), ('rows', 'rep'))  243 us
    reduce_scatter x2, waiting for transfers between devices, aggregate(): lax.psum_scatter(partial_sum.reshape(row_blocks * BS, feature_width).asty...  145 us
    all_gather x2, waiting for transfers between devices, aggregate(): gathered = lax.all_gather(node_field, 'rows', axis=0, tiled=True)  72.1 us
    reduce_scatter x1, waiting for transfers between devices, transpose_aggregate(): lax.psum_scatter(summed.reshape(col_blocks * BS, feature_width).astype(jn...  58.3 us
    all_gather x1, waiting for transfers between devices, transpose_aggregate(): lax.all_gather(cotangent, 'rep', axis=0, tiled=True)  43.4 us
    dot_general x8, matrix products, aggregate(): jnp.einsum('rij,rjf->rif', weights, picked, preferred_element_type=jnp.fl...  15.9 us
    gather x8, local copies, waits for them, and re-layouts, aggregate(): picked = blocks_in[column_ids[:, slot]]  15.5 us
    scatter-add x4, other arithmetic, transpose_aggregate(): summed = summed.at[column_ids[:, slot]].add(terms)  14.1 us
  transfers between devices with their start and end apart: 7, of which 7 were waited for; matrix products, arithmetic and copies ran while one was open for 11% of the time, Pallas kernels for 0%

commit v1 on v0

--- a/solution.py
+++ b/solution.py
@@ -80,7 +80,7 @@
     local_first = lax.dot_general(
         mixed_input, back_pre, contract, preferred_element_type=jnp.float32
     )
-    grad_first, grad_second = lax.psum((local_first, local_second), ("rows", "rep"))
+    grad_first, grad_second = lax.psum(lax.psum((local_first, local_second), "rep"), "rows")
     return (embedding, grad_first * scale_factor, grad_second * scale_factor)
 
 

time: 650 us -> 689 us (1.060)
  waiting for transfers between devices: 563 us -> 608 us
  matrix products: 34.5 us -> 27.2 us
    psum x1 -> x2, waiting for transfers between devices: 243 us -> 282 us  [the longest x1 172 us: shards(): lax.psum((local_first, local_second), 'rep')]
    dot_general x8, matrix products: 15.9 us -> 8.62 us  [aggregate(): jnp.einsum('rij,rjf->rif', weights, picked, preferred_element_type=jnp.fl...]
  transfers between devices with their start and end apart: 7 -> 8, of which waited for: 7 -> 8; matrix products, arithmetic and copies ran while one was open for 11% -> 9% of each run, Pallas kernels for 0% -> 0%
where the time goes in v1:
time: 689 us; the launch traced here: 688 us
  waiting for transfers between devices  608 us (88%)
  matrix products  27.2 us (4%)
  other arithmetic  20.4 us (3%)
  local copies, waits for them, and re-layouts  17.9 us (3%)
  between operations  14.3 us (2%)
    psum x1, waiting for transfers between devices, shards(): lax.psum((local_first, local_second), 'rep')  172 us
    reduce_scatter x2, waiting for transfers between devices, aggregate(): lax.psum_scatter(partial_sum.reshape(row_blocks * BS, feature_width).asty...  150 us
    psum x1, waiting for transfers between devices, shards(): lax.psum(lax.psum((local_first, local_second), 'rep'), 'rows')  110 us
    all_gather x2, waiting for transfers between devices, aggregate(): gathered = lax.all_gather(node_field, 'rows', axis=0, tiled=True)  71.6 us
    reduce_scatter x1, waiting for transfers between devices, transpose_aggregate(): lax.psum_scatter(summed.reshape(col_blocks * BS, feature_width).astype(jn...  59.3 us
    all_gather x1, waiting for transfers between devices, transpose_aggregate(): lax.all_gather(cotangent, 'rep', axis=0, tiled=True)  43.5 us
    gather x8, local copies, waits for them, and re-layouts, aggregate(): picked = blocks_in[column_ids[:, slot]]  15.4 us
    scatter-add x4, other arithmetic, transpose_aggregate(): summed = summed.at[column_ids[:, slot]].add(terms)  14.1 us
  transfers between devices with their start and end apart: 8, of which 8 were waited for; matrix products, arithmetic and copies ran while one was open for 9% of the time, Pallas kernels for 0%

profile of v1, /device:TPU:2, one launch (start us, length us, event | category | flops | bytes accessed | tf_op | source)
XLA Modules:
  0.0 688.3 jit_solution(12731600118760884957)
XLA Ops:
  7.2 0.7 all-gather.4.cloned.1.call-update
  8.0 0.7 all-gather.8.cloned.1.call-update
  8.7 0.8 fusion.10
  9.6 0.7 compare_bitcast_fusion
  10.2 37.3 %all-gather.4.cloned.1.call-done = bf16[2048,256]{1,0:T(8,128)(2,1)} async-done(((bf16[128,256]{1,0:T(8,128)(2,1)}), bf16[2048,256]{1,0:T(8,128)(2,1)}) %all-gather.4.cloned.1.call-update) | async-done | bytes 1048592 | tf_op jit(solution)/shard_map/all_gather | solution.py:18
  47.6 2.9 gather_fusion.2
  50.5 1.6 gather_fusion
  52.1 1.6 gather_fusion.1
  53.7 1.6 gather_fusion.3
  55.3 1.8 fusion.21
  57.1 0.5 fusion.18
  57.6 0.7 copy-done.11
  58.3 0.5 fusion.15
  58.8 0.1 copy-done.7
  58.9 1.6 add_convert_fusion.1
  60.5 43.5 %all-gather.8.cloned.1.call-done = bf16[2048,256]{1,0:T(8,128)(2,1)} async-done(((bf16[128,256]{1,0:T(8,128)(2,1)}), bf16[2048,256]{1,0:T(8,128)(2,1)}) %all-gather.8.cloned.1.call-update) | async-done | bytes 1048592 | tf_op jit(solution)/shard_map/all_gather | solution.py:39
  104.0 3.3 fusion.16
  107.3 0.2 broadcast_in_dim.78
  107.5 3.5 scatter_fusion
  111.1 3.1 fusion.13
  114.2 3.5 scatter_fusion.1
  117.7 3.1 fusion.19
  120.9 3.5 scatter_fusion.2
  124.4 3.1 fusion.22
  127.5 3.5 scatter_fusion.3
  131.0 1.1 convert_element_type.39
  132.2 58.9 %reduce-scatter.4.cloned.1.call-done = bf16[128,256]{1,0:T(8,128)(2,1)} async-done(((bf16[2048,256]{1,0:T(8,128)(2,1)}), bf16[128,256]{1,0:T(8,128)(2,1)}) %reduce-scatter.4.cloned.1.call-update) | async-done | bytes 65552 | tf_op jit(solution)/shard_map/reduce_scatter | solution.py:28
  191.1 1.0 fusion.23
  192.1 59.3 %reduce-scatter.8.cloned.1.call-done = bf16[128,256]{1,0:T(8,128)(2,1)} async-done(((bf16[2048,256]{1,0:T(8,128)(2,1)}), bf16[128,256]{1,0:T(8,128)(2,1)}) %reduce-scatter.8.cloned.1.call-update) | async-done | bytes 65552 | tf_op jit(solution)/shard_map/reduce_scatter | solution.py:48
  251.5 1.9 fusion.12
  253.4 2.1 fusion.2
  255.6 0.8 convolution_convert_fusion
  256.5 171.8 %all-reduce.5.cloned.1.call-done = (f32[256,512]{1,0:T(8,128)}, f32[512,256]{1,0:T(8,128)}) async-done(((f32[256,512]{1,0:T(8,128)}, f32[512,256]{1,0:T(8,128)}), (f32[256,512]{1,0:T(8,128)}, f32[512,256]{1,0:T(8,128)})) %all-reduce.5.cloned.1.call-update) | async-done | bytes 1048592 | tf_op jit(solution)/shard_map/psum | solution.py:83
  428.3 34.3 %all-gather.6.cloned.1.call-done = bf16[2048,256]{1,0:T(8,128)(2,1)} async-done(((bf16[128,256]{1,0:T(8,128)(2,1)}), bf16[2048,256]{1,0:T(8,128)(2,1)}) %all-gather.6.cloned.1.call-update) | async-done | bytes 1048592 | tf_op jit(solution)/shard_map/all_gather | solution.py:18
  462.6 2.9 gather_fusion.6
  465.5 1.6 gather_fusion.4
  467.2 1.6 gather_fusion.5
  468.7 1.6 gather_fusion.7
  470.4 1.8 fusion.20
  472.2 0.5 fusion.17
  472.7 0.7 copy-done.8
  473.4 0.5 fusion.14
  473.9 0.7 copy-done.6
  474.6 1.5 add_convert_fusion
  476.2 110.5 %all-reduce.7.cloned.1.call-done = (f32[256,512]{1,0:T(8,128)}, f32[512,256]{1,0:T(8,128)}) async-done(((f32[256,512]{1,0:T(8,128)}, f32[512,256]{1,0:T(8,128)}), (f32[256,512]{1,0:T(8,128)}, f32[512,256]{1,0:T(8,128)})) %all-reduce.7.cloned.1.call-update) | async-done | bytes 1048592 | tf_op jit(solution)/shard_map/psum | solution.py:83
  586.6 1.9 broadcast_multiply_fusion.1
  588.5 1.9 broadcast_multiply_fusion
  590.4 91.1 %reduce-scatter.6.cloned.1.call-done = bf16[128,256]{1,0:T(8,128)(2,1)} async-done(((bf16[2048,256]{1,0:T(8,128)(2,1)}), bf16[128,256]{1,0:T(8,128)(2,1)}) %reduce-scatter.6.cloned.1.call-update) | async-done | bytes 65552 | tf_op jit(solution)/shard_map/reduce_scatter | solution.py:28
  (38 shorter events, 0.5 us)
Async XLA Ops:
  7.2 246.2 %copy-start = (bf16[512,256]{1,0:T(8,128)(2,1)S(1)}, bf16[512,256]{1,0:T(8,128)(2,1)}, u32[]{:S(2)}) copy-start(bf16[512,256]{1,0:T(8,128)(2,1)} %param.12) | copy-start | bytes 786436
  7.2 40.4 %all-gather.4.cloned.1.call-start = ((), (), s32[]{:S(2)}) async-start(), calls=%async_computation.3 | async-start | bytes 1114112 | tf_op jit(solution)/shard_map/all_gather | solution.py:18
  7.9 96.1 %all-gather.8.cloned.1.call-start = ((), (), s32[]{:S(2)}) async-start(), calls=%async_computation.7 | async-start | bytes 1114112 | tf_op jit(solution)/shard_map/all_gather | solution.py:39
  8.7 182.4 %reduce-scatter.4.cloned.1.call-start = ((), (), s32[]{:S(2)}) async-start(), calls=%async_computation.4 | async-start | bytes 1114112 | tf_op jit(solution)/shard_map/reduce_scatter | solution.py:28
  47.6 2.9 copy-start.3
  52.1 3.2 copy-start.1
  55.3 1.8 copy-start.10
  57.1 1.2 copy-start.11
  57.6 1.3 copy-start.7
  60.5 191.0 %reduce-scatter.8.cloned.1.call-start = ((), (), s32[]{:S(2)}) async-start(), calls=%async_computation.8 | async-start | bytes 1114112 | tf_op jit(solution)/shard_map/reduce_scatter | solution.py:48
  107.5 3.5 copy-start.5
  131.0 60.1 %copy-start.12 = (bf16[256,512]{1,0:T(8,128)(2,1)S(1)}, bf16[256,512]{1,0:T(8,128)(2,1)}, u32[]{:S(2)}) copy-start(bf16[256,512]{1,0:T(8,128)(2,1)} %param.11) | copy-start | bytes 786436
  132.2 296.1 %all-reduce.5.cloned.1.call-start = ((), (), s32[]{:S(2)}) async-start(), calls=%async_computation.9 | async-start | bytes 2097152 | tf_op jit(solution)/shard_map/psum | solution.py:83
  255.5 207.1 %all-gather.6.cloned.1.call-start = ((), (), s32[]{:S(2)}) async-start(), calls=%async_computation.5 | async-start | bytes 1114112 | tf_op jit(solution)/shard_map/all_gather | solution.py:18
  256.4 330.2 %all-reduce.7.cloned.1.call-start = ((), (), s32[]{:S(2)}) async-start(), calls=%async_computation.10 | async-start | bytes 2097152 | tf_op jit(solution)/shard_map/psum | solution.py:83
  428.3 253.2 %reduce-scatter.6.cloned.1.call-start = ((), (), s32[]{:S(2)}) async-start(), calls=%async_computation.6 | async-start | bytes 1114112 | tf_op jit(solution)/shard_map/reduce_scatter | solution.py:28
  462.6 2.9 copy-start.4
  467.1 3.2 copy-start.2
  470.3 1.8 copy-start.9
  472.2 1.2 copy-start.8
  473.4 1.2 copy-start.6
Sparse Core Ops, SparseCore 0:
  9.9 37.6 all-gather.3
  50.0 53.9 all-gather.7
  107.5 83.5 reduce-scatter.3
  193.6 57.7 reduce-scatter.7
  255.6 172.5 all-reduce.4
  430.7 31.8 all-gather.5
  465.5 121.0 all-reduce.6
  590.7 90.7 reduce-scatter.5
